TPU v7x, 32 devices: a whole 2x2x4 slice. The times are simulated.
32 devices in a mesh: gx: 4 (over x, core), gy: 2 (over y), gz: 4 (over z).
Axes of the slice: x: 2, y: 2, z: 4, core: 2. Of those that a mesh axis runs over, the one named last changes fastest.
Arguments:
- spline_weights: bfloat16 [256, 256, 128], P(('gx', 'gy', 'gz')), may hold values from 0 to 0.125
- point_source: float32 [256, 256], P(('gx', 'gy', 'gz')), may hold values from -6 to 6
- confidence: float32 [256, 256], P(('gx', 'gy', 'gz')), may hold values from 0.25 to 4
- block_dest: int32 [256, 1], P(('gx', 'gy', 'gz')), may hold values from 0 to 7; in each aligned block of 8 rows (0 to 7, 8 to 15, ...) at most 2 rows name the same one
- offsets: int32 [3, 256], P(None, ('gx', 'gy', 'gz')), may hold values from 0 to 120, as said below
- block_count: int32 [32], P(('gx', 'gy', 'gz')), may hold values from 4 to 8, as said below
Outputs:
- solution_field: float32 [32, 16, 512], P('gx', 'gy', 'gz')
- residual: float32 [32, 16, 512], P('gx', 'gy', 'gz')
- point_field: float32 [256, 256], P(('gx', 'gy', 'gz'))
Inputs may be any that keep to these rules, and one draw needn't show every extreme that they name: `block_dest`: among the 8 slots of each device at most 2 name one brick, a bound that some block reaches of them. `offsets`: rows 0, 1 and 2 lie in 0 to 4, 0 to 4, 0 to 120, so a patch never leaves its brick; each end is reached. `block_count`: some device has all 8 slots live.
All inputs are finite; a program needn't handle non-finite values.
Results may differ from a plain program's by a relative error of at most 0.0003.
Values sent between devices are 32-bit elements; how exact they have to be, the bound alone decides.
A program may use at most 64 MiB of HBM per device.

v0:
```python
import functools
import jax
import jax.numpy as jnp
from jax import lax
from jax.experimental import pallas as pl
from jax.experimental.pallas import tpu as pltpu
from jax.sharding import PartitionSpec as P

BX = 8
BY = 8
BZ = 128
PX = 4
PY = 4
PZ = 8
ITERS = 3
MESH = pl.DeviceIdType.MESH
F32 = jnp.float32
BF16 = jnp.bfloat16
HI = lax.Precision.HIGHEST
DIRS = [
    (dx, dy, dz)
    for dx in (-1, 0, 1)
    for dy in (-1, 0, 1)
    for dz in (-1, 0, 1)
    if (dx, dy, dz) != (0, 0, 0)
]


def code(dx, dy, dz):
    return (dx + 1) * 9 + (dy + 1) * 3 + (dz + 1)


def halves(value):
    high = value.astype(BF16)
    return high, (value - high.astype(F32)).astype(BF16)


def iota(shape, dim):
    return lax.broadcasted_iota(jnp.int32, shape, dim)


def repeat(count, body, init):
    if count <= 8:
        for i in range(count):
            init = body(i, init)
        return init
    return lax.fori_loop(0, count, body, init)


def smooth(v):
    n = v.shape[0]
    v = v[1 : n - 1] + 0.5 * (v[: n - 2] + v[2:])
    v = v + 0.5 * (pltpu.roll(v, 1, 1) + pltpu.roll(v, 15, 1))
    return v + 0.5 * (pltpu.roll(v, 1, 2) + pltpu.roll(v, 255, 2))


def coefficients(m):
    def add(p, a, q):
        out = []
        for i in range(max(len(p), len(q))):
            left = p[i] if i < len(p) else None
            right = a * q[i] if i < len(q) else None
            out.append(right if left is None else left if right is None else left + right)
        return out

    def form(p, q):
        total = None
        for i in range(len(p)):
            for j in range(len(q)):
                term = p[i] * q[j] * m[i + j]
                total = term if total is None else total + term
        return total

    one = jnp.ones_like(m[0])
    direction, residual, field = [one], [one], []
    now = m[0]
    for step in range(ITERS):
        image = [16.0 * c for c in direction] + [jnp.zeros_like(one)]
        image = [image[i] + (16.0 * direction[i - 1] if i else 0.0) for i in range(len(image))]
        alpha = now / form(direction, image)
        field = add(field, alpha, direction)
        residual = add(residual, -alpha, image)
        if step + 1 < ITERS:
            new = form(residual, residual)
            direction = add(residual, new / now, direction)
            now = new
    return field, residual


def kernel(sizes, count_ref, w_hbm, src_hbm, conf_hbm, dest_hbm, off_hbm,
           field_ref, resid_ref, point_ref,
           send, recv, zhot, fbuf, ylow, yhigh, zpack, zrecv, yrecv, erecv, xrecv,
           part, parts, colpart, colparts, back, returned, pay,
           w_ref, src_ref, conf_ref, dest_ref, off_ref, in_s, a_s, a_r, h_s, h_r, g_s, g_r, c_s, c_r, b_s, b_r):
    nx, ny, nz, slots, cap = sizes
    group = ny * nz
    gx, gy, gz = lax.axis_index("gx"), lax.axis_index("gy"), lax.axis_index("gz")
    me = gy * nz + gz

    def peer(d):
        other = lax.rem(me + d, group)
        return other, (gx, lax.div(other, nz), lax.rem(other, nz))

    def sender(d):
        return lax.rem(me + group - d, group)

    def exists(dx, dy, dz):
        ok = None
        for d, g, n in ((dx, gx, nx), (dy, gy, ny), (dz, gz, nz)):
            if d:
                this = g + 1 < n if d > 0 else g > 0
                ok = this if ok is None else jnp.logical_and(ok, this)
        return ok

    loads = [
        pltpu.make_async_copy(a, b, in_s.at[i])
        for i, (a, b) in enumerate(
            ((dest_hbm, dest_ref), (off_hbm, off_ref), (src_hbm, src_ref), (conf_hbm, conf_ref), (w_hbm, w_ref))
        )
    ]
    for c in loads:
        c.start()
    zrecv[...] = jnp.zeros_like(zrecv)
    yrecv[...] = jnp.zeros_like(yrecv)
    erecv[...] = jnp.zeros_like(erecv)
    xrecv[...] = jnp.zeros_like(xrecv)

    barrier = pltpu.get_barrier_semaphore()
    for d in range(1, group):
        pl.semaphore_signal(barrier, inc=1, device_id=peer(d)[1], device_id_type=MESH)
    for d in range(1, nx):
        pl.semaphore_signal(barrier, inc=1, device_id=(lax.rem(gx + d, nx), gy, gz), device_id_type=MESH)
    for dx, dy, dz in DIRS:
        if dx and (dy or dz):
            @pl.when(exists(dx, dy, dz))
            def _():
                pl.semaphore_signal(barrier, inc=1, device_id=(gx + dx, gy + dy, gz + dz), device_id_type=MESH)

    loads[0].wait()
    loads[1].wait()
    live_count = count_ref[0]
    row_n, lane_n = iota((slots, slots), 0), iota((slots, slots), 1)
    eye = row_n == lane_n
    drow = dest_ref[...].astype(F32)
    dcol = jnp.sum(jnp.where(eye, drow, 0.0), axis=1, keepdims=True)
    earlier = (dcol == drow) & (lane_n < row_n) & (lane_n < live_count)
    rank = jnp.sum(jnp.where(earlier, 1.0, 0.0), axis=1, keepdims=True)
    tcol = jnp.where(iota((slots, 1), 0) < live_count, dcol * cap + rank, -1.0)
    off = off_ref[...].astype(F32)
    zcol = jnp.sum(jnp.where(eye, off[2:3], 0.0), axis=1, keepdims=True)
    xycol = jnp.sum(jnp.where(eye, off[0:1] * BY + off[1:2], 0.0), axis=1, keepdims=True)
    pay[2 * slots : 3 * slots, :] = jnp.broadcast_to(zcol, (slots, 128))
    pay[3 * slots : 4 * slots, :] = jnp.broadcast_to(xycol, (slots, 128))
    lanes = iota((slots, 4 * slots), 1)
    trow = jnp.sum(
        jnp.where(iota((slots, 4 * slots), 0) == lax.rem(lanes, slots), tcol, 0.0), axis=0, keepdims=True
    )
    rows = 4 * cap
    tr = iota((group * rows, 4 * slots), 0)
    tl = iota((group * rows, 4 * slots), 1)
    inner = lax.rem(tr, rows)
    want = (lax.div(tr, rows) * cap + lax.rem(inner, cap)).astype(F32)
    sel = jnp.where((lax.div(inner, cap) == lax.div(tl, slots)) & (want == trow), 1.0, 0.0)
    for c in loads[2:]:
        c.wait()
    s_hi, s_lo = halves(src_ref[...])
    c_hi, c_lo = halves(conf_ref[...])
    left_s = jnp.concatenate([s_hi, s_lo], 0)
    left_c = jnp.concatenate([c_hi, c_lo], 0)
    for n in range(slots):
        w = w_ref[n]
        wf = w.astype(F32)
        q_hi, q_lo = halves(wf * wf)
        rhs = jnp.dot(left_s, w, preferred_element_type=F32)
        den = jnp.dot(left_c, q_hi, preferred_element_type=F32) + jnp.dot(
            left_c, q_lo, preferred_element_type=F32
        )
        pay[n : n + 1, :] = rhs[n : n + 1] + rhs[slots + n : slots + n + 1]
        pay[slots + n : slots + n + 1, :] = den[n : n + 1] + den[slots + n : slots + n + 1]

    send[...] = jnp.dot(sel, pay[...], precision=HI, preferred_element_type=F32).reshape(group, rows, 128)
    recv[me] = send[me]

    near = [jnp.minimum(g, 1) + jnp.minimum(n - 1 - g, 1) for g, n in ((gx, nx), (gy, ny), (gz, nz))]
    diagonal = near[0] * ((near[1] + 1) * (near[2] + 1) - 1)
    pl.semaphore_wait(barrier, group - 1 + nx - 1 + diagonal)

    def to_group(src_of, dst, ssem, rsem):
        copies = []
        for d in range(1, group):
            other, where = peer(d)
            c = pltpu.make_async_remote_copy(
                src_ref=src_of(other), dst_ref=dst.at[me], send_sem=ssem.at[d], recv_sem=rsem.at[d],
                device_id=where, device_id_type=MESH,
            )
            c.start()
            copies.append(c)
        return copies

    def from_group(dst, ssem, rsem):
        for d in range(1, group):
            q = sender(d)
            pltpu.make_async_remote_copy(
                src_ref=dst.at[q], dst_ref=dst.at[q], send_sem=ssem.at[d], recv_sem=rsem.at[d],
                device_id=peer(d)[1], device_id_type=MESH,
            ).wait_recv()

    sent = to_group(lambda other: send.at[other], recv, a_s, a_r)
    from_group(recv, a_s, a_r)

    cell = iota((BX * BY, 128), 1)
    place_xy = (iota((BX * BY, 128), 0) - (lax.shift_right_logical(cell, 5) * BY + (lax.shift_right_logical(cell, 3) & 3))).astype(F32)
    place_z = (iota((128, BZ), 1) - (iota((128, BZ), 0) & 7)).astype(F32)

    def scatter(g, acc):
        got = recv[g]
        lefts, hots = [], []
        for k in range(cap):
            hot = jnp.where(place_z == got[2 * cap + k : 2 * cap + k + 1], 1.0, 0.0).astype(BF16)
            hots.append(hot)
            at = place_xy == got[3 * cap + k : 3 * cap + k + 1]
            values = jnp.concatenate(
                [jnp.where(at, got[k : k + 1], 0.0), jnp.where(at, got[cap + k : cap + k + 1], 0.0)], 0
            )
            lefts.append(jnp.concatenate(halves(values), 0))
        hot = jnp.concatenate(hots, 0)
        zhot[g] = hot
        return acc + jnp.dot(jnp.concatenate(lefts, 1), hot, preferred_element_type=F32)

    acc = repeat(group, scatter, jnp.zeros((4 * BX * BY, BZ), F32))
    both = acc[: 2 * BX * BY] + acc[2 * BX * BY :]
    rhs = both[: BX * BY].reshape(BX, BY, BZ)
    den = (0.25 * both[BX * BY :]).reshape(BX, BY, BZ)

    lane = iota((BY, BZ), 1)
    sub = iota((BY, BZ), 0)
    rim = (lane < 3) | (lane >= BZ - 3)
    packed = jnp.zeros((BY, BZ), F32)
    for f, field in enumerate((rhs, den)):
        for x in range(BX):
            edge = jnp.where(rim, field[x], 0.0)
            shift = 8 * x + 64 * f
            packed = packed + (pltpu.roll(edge, shift, 1) if shift else edge)
            fbuf[x, f] = field[x]
        for j in range(BX // 2):
            even, odd = field[2 * j], pltpu.roll(field[2 * j + 1], 4, 0)
            ylow[j, f] = jnp.where(sub < 4, even, odd)
            yhigh[j, f] = jnp.where(sub < 4, odd, even)
    zpack[...] = packed

    def buffers(dx, dy, dz):
        if dz:
            return zpack, zrecv.at[code(-dx, -dy, -dz)]
        if dy:
            source = ylow if dy < 0 else yhigh
            side = 0 if dy > 0 else 1
            if not dx:
                return source, yrecv.at[side]
            return source.at[pl.ds(2 if dx > 0 else 0, 2)], erecv.at[0 if dx > 0 else 1, side]
        return fbuf.at[pl.ds(5 if dx > 0 else 0, 3)], xrecv.at[0 if dx > 0 else 1]

    def halo(dx, dy, dz):
        source, target = buffers(dx, dy, dz)
        return pltpu.make_async_remote_copy(
            src_ref=source, dst_ref=target,
            send_sem=h_s.at[code(dx, dy, dz)], recv_sem=h_r.at[code(-dx, -dy, -dz)],
            device_id=(gx + dx, gy + dy, gz + dz), device_id_type=MESH,
        )

    order = sorted(DIRS, key=lambda d: (d[2] != 0, d[0] != 0))
    for d in order:
        @pl.when(exists(*d))
        def _():
            halo(*d).start()
    for c in sent:
        c.wait_send()
    for d in order:
        @pl.when(exists(*d))
        def _():
            dx, dy, dz = d
            halo(-dx, -dy, -dz).wait_recv()

    def rim_pack(dx, dy):
        return jnp.where((lane & 7) < 4, zrecv[code(dx, dy, 1)], zrecv[code(dx, dy, -1)])

    fields = [[], []]
    for dx, xs in ((-1, (5, 6, 7)), (0, tuple(range(BX))), (1, (0, 1, 2))):
        pack0 = rim_pack(dx, 0)
        pack1 = jnp.where(sub < 4, rim_pack(dx, 1), rim_pack(dx, -1))
        for i, x in enumerate(xs):
            for f in range(2):
                if dx:
                    side = 0 if dx < 0 else 1
                    own = xrecv[side, i, f]
                    pair = x // 2 - (2 if dx < 0 else 0)
                    low, high = erecv[side, 1, pair, f], erecv[side, 0, pair, f]
                else:
                    own = fbuf[x, f]
                    low, high = yrecv[1, x // 2, f], yrecv[0, x // 2, f]
                if x % 2 == 0:
                    beside = jnp.where(sub < 4, low, high)
                else:
                    beside = pltpu.roll(jnp.where(sub < 4, high, low), 4, 0)
                shift = (BZ - 8 * x - 64 * f) % BZ
                z0 = jnp.where(rim, pltpu.roll(pack0, shift, 1) if shift else pack0, 0.0)
                z1 = jnp.where(rim, pltpu.roll(pack1, shift, 1) if shift else pack1, 0.0)
                top = jnp.concatenate([own, z0], 1)
                low_rows = jnp.concatenate([beside, z1], 1)
                fields[f].append(jnp.concatenate([top, low_rows], 0))
    v0, dens = jnp.stack(fields[0]), jnp.stack(fields[1])

    ry, rz = iota((16, 256), 0), iota((16, 256), 1)
    yes = ((ry < 8) | ((ry < 12) & (gy + 1 < ny)) | ((ry >= 12) & (gy > 0))) & (
        (rz < 128) | ((rz < 192) & (gz + 1 < nz)) | ((rz >= 192) & (gz > 0))
    )
    inside = jnp.where(yes, 1.0, 0.0)
    before = inside * jnp.where(gx > 0, 1.0, 0.0)
    after = inside * jnp.where(gx + 1 < nx, 1.0, 0.0)

    def step(v, depth):
        out = dens[depth : 14 - depth] * v[1:-1] - 0.125 * smooth(v)
        rims = 3 - depth
        masks = [before] * rims + [inside] * BX + [after] * rims
        return out * jnp.stack(masks) if rims else out

    v1 = step(v0, 1)
    v2 = step(v1, 2)
    v3 = step(v2, 3)
    basis = [rhs, v1[2:10, :8, :128], v2[1:9, :8, :128], v3[:, :8, :128]]
    lines = []
    for k in range(2 * ITERS):
        product = jnp.sum(basis[k // 2] * basis[(k + 1) // 2], axis=0)
        lines.append(jnp.sum(product, axis=0, keepdims=True))
    lines.append(jnp.zeros((2, 128), F32))
    part[...] = jnp.concatenate(lines, 0)
    parts[me] = part[...]
    sent = to_group(lambda other: part, parts, g_s, g_r)
    for d in order:
        @pl.when(exists(*d))
        def _():
            halo(*d).wait_send()
    from_group(parts, g_s, g_r)
    total = repeat(group, lambda g, t: t + parts[g], jnp.zeros((8, 128), F32))
    colpart[...] = total
    colparts[gx] = total
    col = []
    for d in range(1, nx):
        c = pltpu.make_async_remote_copy(
            src_ref=colpart, dst_ref=colparts.at[gx], send_sem=c_s.at[d], recv_sem=c_r.at[d],
            device_id=(lax.rem(gx + d, nx), gy, gz), device_id_type=MESH,
        )
        c.start()
        col.append(c)
    for d in range(1, nx):
        q = lax.rem(gx + nx - d, nx)
        pltpu.make_async_remote_copy(
            src_ref=colpart, dst_ref=colparts.at[q], send_sem=c_s.at[d], recv_sem=c_r.at[d],
            device_id=(lax.rem(gx + d, nx), gy, gz), device_id_type=MESH,
        ).wait_recv()
    total = repeat(nx, lambda g, t: t + colparts[g], jnp.zeros((8, 128), F32))
    moments = jnp.broadcast_to(jnp.sum(total, axis=1, keepdims=True), (8, 128))
    field_c, resid_c = coefficients([moments[k : k + 1] for k in range(2 * ITERS)])

    def combine(cs):
        out = None
        for c, v in zip(cs, basis):
            term = c.reshape(1, 1, 128) * v
            out = term if out is None else out + term
        return out

    field = combine(field_c)
    field_ref[...] = field
    flat = jnp.concatenate(halves(field.reshape(BX * BY, BZ)), 0)

    def gather(g, carry):
        picked = lax.dot_general(flat, zhot[g], (((1,), (1,)), ((), ())), preferred_element_type=F32)
        picked = picked[: BX * BY] + picked[BX * BY :]
        got = recv[g]
        lines = []
        for k in range(cap):
            at = place_xy == got[3 * cap + k : 3 * cap + k + 1]
            lines.append(
                jnp.sum(jnp.where(at, picked[:, 128 * k : 128 * k + 128], 0.0), axis=0, keepdims=True)
            )
        lines.append(jnp.zeros((rows - cap, 128), F32))
        back[g] = jnp.concatenate(lines, 0)
        return carry

    repeat(group, gather, 0)
    returned[me] = back[me]
    last = to_group(lambda other: back.at[other], returned, b_s, b_r)
    resid_ref[...] = combine(resid_c)
    for c in sent + col:
        c.wait_send()
    tr = iota((slots, group * rows), 1)
    inner = lax.rem(tr, rows)
    want = (lax.div(tr, rows) * cap + inner).astype(F32)
    sel = jnp.where((inner < cap) & (want == tcol), 1.0, 0.0)
    from_group(returned, b_s, b_r)
    values = jnp.dot(sel, returned[...].reshape(group * rows, 128), precision=HI, preferred_element_type=F32)
    left = jnp.concatenate(halves(values), 0)
    for n in range(slots):
        out = lax.dot_general(left, w_ref[n], (((1,), (1,)), ((), ())), preferred_element_type=F32)
        point_ref[n : n + 1, :] = out[n : n + 1] + out[slots + n : slots + n + 1]
    for c in last:
        c.wait_send()


def shards(nx, ny, nz, spline_weights, point_source, confidence, block_dest, offsets, block_count):
    slots, points, patch = spline_weights.shape
    group = ny * nz
    cap = max(2, (slots + group - 1) // group)
    rows = 4 * cap
    vmem = pl.BlockSpec(memory_space=pltpu.VMEM)
    dma = pltpu.SemaphoreType.DMA
    return pl.pallas_call(
        functools.partial(kernel, (nx, ny, nz, slots, cap)),
        out_shape=(
            jax.ShapeDtypeStruct((BX, BY, BZ), F32),
            jax.ShapeDtypeStruct((BX, BY, BZ), F32),
            jax.ShapeDtypeStruct((slots, points), F32),
        ),
        in_specs=[pl.BlockSpec(memory_space=pltpu.SMEM)] + [pl.BlockSpec(memory_space=pltpu.HBM)] * 5,
        out_specs=(vmem, vmem, vmem),
        scratch_shapes=[
            pltpu.VMEM((group, rows, 128), F32),
            pltpu.VMEM((group, rows, 128), F32),
            pltpu.VMEM((group, cap * 128, BZ), BF16),
            pltpu.VMEM((BX, 2, BY, BZ), F32),
            pltpu.VMEM((BX // 2, 2, BY, BZ), F32),
            pltpu.VMEM((BX // 2, 2, BY, BZ), F32),
            pltpu.VMEM((BY, BZ), F32),
            pltpu.VMEM((27, BY, BZ), F32),
            pltpu.VMEM((2, BX // 2, 2, BY, BZ), F32),
            pltpu.VMEM((2, 2, 2, 2, BY, BZ), F32),
            pltpu.VMEM((2, 3, 2, BY, BZ), F32),
            pltpu.VMEM((8, 128), F32),
            pltpu.VMEM((group, 8, 128), F32),
            pltpu.VMEM((8, 128), F32),
            pltpu.VMEM((nx, 8, 128), F32),
            pltpu.VMEM((group, rows, 128), F32),
            pltpu.VMEM((group, rows, 128), F32),
            pltpu.VMEM((4 * slots, 128), F32),
            pltpu.VMEM(spline_weights.shape, BF16),
            pltpu.VMEM(point_source.shape, F32),
            pltpu.VMEM(confidence.shape, F32),
            pltpu.VMEM((1, slots), jnp.int32),
            pltpu.VMEM(offsets.shape, jnp.int32),
            dma((5,)),
            dma((group,)), dma((group,)), dma((27,)), dma((27,)), dma((group,)), dma((group,)),
            dma((nx,)), dma((nx,)), dma((group,)), dma((group,)),
        ],
        compiler_params=pltpu.CompilerParams(
            collective_id=0, has_side_effects=True, vmem_limit_bytes=40 * 1024 * 1024
        ),
    )(
        block_count,
        *(
            pltpu.with_memory_space_constraint(a, pltpu.HBM)
            for a in (spline_weights, point_source, confidence, block_dest.reshape(1, slots), offsets)
        ),
    )


def solution(mesh):
    sizes = (mesh.shape["gx"], mesh.shape["gy"], mesh.shape["gz"])
    return jax.shard_map(
        functools.partial(shards, *sizes),
        mesh=mesh,
        in_specs=(
            P(("gx", "gy", "gz"), None, None),
            P(("gx", "gy", "gz"), None),
            P(("gx", "gy", "gz"), None),
            P(("gx", "gy", "gz"), None),
            P(None, ("gx", "gy", "gz")),
            P(("gx", "gy", "gz")),
        ),
        out_specs=(P("gx", "gy", "gz"), P("gx", "gy", "gz"), P(("gx", "gy", "gz"), None)),
        check_vma=False,
    )
```

profile of v0, /device:TPU:0, one launch (start us, length us, event | category | flops | bytes accessed | tf_op | source)
XLA Modules:
  0.0 29.8 jit_solution(11743266258746086652)
XLA Ops:
  1.3 26.7 %shard_map.85 = (f32[8,8,128]{2,1,0:T(8,128)S(1)}, f32[8,8,128]{2,1,0:T(8,128)S(1)}, f32[8,256]{1,0:T(8,128)S(1)}) custom-call(s32[1]{0:T(128)S(6)} %copy.12.count_ref, bf16[8,256,128]{2,1,0:T(8,128)(2,1)} %w_hbm.1, f32[8,256]{1,0:T(8,128)} %src_hbm.1, f32[8,256]{1,0:T(8,128)} %conf_hbm.1, s32[1,8]{1,0:T(1,128)} %bitcast.1, s32[3,8]{1,0:T(4,128)} %off_hbm.1), custom_call_target="tpu_custom_call" | custom-call | tf_op jit(solution)/shard_map/pallas_call | solution.py:416
  28.0 0.6 %copy.13 = f32[8,8,128]{2,1,0:T(8,128)} copy(f32[8,8,128]{2,1,0:T(8,128)S(1)} %get-tuple-element.6) | data formatting | bytes 65536
  28.6 0.6 %copy.14 = f32[8,8,128]{2,1,0:T(8,128)} copy(f32[8,8,128]{2,1,0:T(8,128)S(1)} %get-tuple-element.7) | data formatting | bytes 65536
  29.2 0.6 %copy.15 = f32[8,256]{1,0:T(8,128)} copy(f32[8,256]{1,0:T(8,128)S(1)} %get-tuple-element.8) | data formatting | bytes 16384
where the time goes:
time: 30 us; the launch traced here: 29.8 us
  Pallas kernels  26.7 us (89%)
  local copies, waits for them, and re-layouts  1.83 us (6%)
  between operations  1.29 us (4%)
    pallas_call x1, Pallas kernels, shards(): pl.pallas_call(functools.partial(kernel, (nx, ny, nz, slots, cap)), out_s...  26.7 us
    unnamed x3, local copies, waits for them, and re-layouts  1.83 us

commit v1 on v0

--- a/solution.py
+++ b/solution.py
@@ -87,22 +87,40 @@
     return field, residual
 
 
-def kernel(sizes, count_ref, w_hbm, src_hbm, conf_hbm, dest_hbm, off_hbm,
+def kernel(sizes, w_hbm, src_hbm, conf_hbm, dest_hbm, off_hbm, count_hbm,
            field_ref, resid_ref, point_ref,
            send, recv, zhot, fbuf, ylow, yhigh, zpack, zrecv, yrecv, erecv, xrecv,
-           part, parts, colpart, colparts, back, returned, pay,
-           w_ref, src_ref, conf_ref, dest_ref, off_ref, in_s, a_s, a_r, h_s, h_r, g_s, g_r, c_s, c_r, b_s, b_r):
+           part, parts, colpart, colparts, back, returned, pay, values_at,
+           w_ref, src_ref, conf_ref, dest_ref, off_ref, in_s, h_s, h_r, one_s, one_r):
     nx, ny, nz, slots, cap = sizes
     group = ny * nz
     gx, gy, gz = lax.axis_index("gx"), lax.axis_index("gy"), lax.axis_index("gz")
     me = gy * nz + gz
 
-    def peer(d):
-        other = lax.rem(me + d, group)
-        return other, (gx, lax.div(other, nz), lax.rem(other, nz))
-
-    def sender(d):
-        return lax.rem(me + group - d, group)
+    def ring(g, n):
+        return [g] + [lax.rem(g + d, n) for d in range(1, n)]
+
+    xs, ys, zs = ring(gx, nx), ring(gy, ny), ring(gz, nz)
+    in_group = [(y * nz + z, (gx, y, z)) for y in ys for z in zs][1:]
+    in_column = [(x, (x, gy, gz)) for x in xs][1:]
+    everyone = [((x * ny + y) * nz + z, (x, y, z)) for x in xs for y in ys for z in zs][1:]
+
+    def spread(kind, peers, src_of, dst, slot):
+        copies = []
+        for other, where in peers:
+            c = pltpu.make_async_remote_copy(
+                src_ref=src_of(other), dst_ref=dst.at[slot], send_sem=one_s.at[kind], recv_sem=one_r.at[kind],
+                device_id=where, device_id_type=MESH,
+            )
+            c.start()
+            copies.append(c)
+
+    def whole(kind, peers, dst):
+        ref = dst.at[pl.ds(0, len(peers))]
+        return pltpu.make_async_remote_copy(
+            src_ref=ref, dst_ref=ref, send_sem=one_s.at[kind], recv_sem=one_r.at[kind],
+            device_id=peers[0][1], device_id_type=MESH,
+        )
 
     def exists(dx, dy, dz):
         ok = None
@@ -115,7 +133,10 @@
     loads = [
         pltpu.make_async_copy(a, b, in_s.at[i])
         for i, (a, b) in enumerate(
-            ((dest_hbm, dest_ref), (off_hbm, off_ref), (src_hbm, src_ref), (conf_hbm, conf_ref), (w_hbm, w_ref))
+            (
+                (dest_hbm, dest_ref), (off_hbm, off_ref),
+                (src_hbm, src_ref), (conf_hbm, conf_ref), (w_hbm, w_ref),
+            )
         )
     ]
     for c in loads:
@@ -126,19 +147,12 @@
     xrecv[...] = jnp.zeros_like(xrecv)
 
     barrier = pltpu.get_barrier_semaphore()
-    for d in range(1, group):
-        pl.semaphore_signal(barrier, inc=1, device_id=peer(d)[1], device_id_type=MESH)
-    for d in range(1, nx):
-        pl.semaphore_signal(barrier, inc=1, device_id=(lax.rem(gx + d, nx), gy, gz), device_id_type=MESH)
-    for dx, dy, dz in DIRS:
-        if dx and (dy or dz):
-            @pl.when(exists(dx, dy, dz))
-            def _():
-                pl.semaphore_signal(barrier, inc=1, device_id=(gx + dx, gy + dy, gz + dz), device_id_type=MESH)
-
-    loads[0].wait()
-    loads[1].wait()
-    live_count = count_ref[0]
+    for _, where in in_group + in_column:
+        pl.semaphore_signal(barrier, inc=1, device_id=where, device_id_type=MESH)
+
+    for c in loads[:2]:
+        c.wait()
+    live_count = count_hbm[0]
     row_n, lane_n = iota((slots, slots), 0), iota((slots, slots), 1)
     eye = row_n == lane_n
     drow = dest_ref[...].astype(F32)
@@ -181,32 +195,9 @@
     send[...] = jnp.dot(sel, pay[...], precision=HI, preferred_element_type=F32).reshape(group, rows, 128)
     recv[me] = send[me]
 
-    near = [jnp.minimum(g, 1) + jnp.minimum(n - 1 - g, 1) for g, n in ((gx, nx), (gy, ny), (gz, nz))]
-    diagonal = near[0] * ((near[1] + 1) * (near[2] + 1) - 1)
-    pl.semaphore_wait(barrier, group - 1 + nx - 1 + diagonal)
-
-    def to_group(src_of, dst, ssem, rsem):
-        copies = []
-        for d in range(1, group):
-            other, where = peer(d)
-            c = pltpu.make_async_remote_copy(
-                src_ref=src_of(other), dst_ref=dst.at[me], send_sem=ssem.at[d], recv_sem=rsem.at[d],
-                device_id=where, device_id_type=MESH,
-            )
-            c.start()
-            copies.append(c)
-        return copies
-
-    def from_group(dst, ssem, rsem):
-        for d in range(1, group):
-            q = sender(d)
-            pltpu.make_async_remote_copy(
-                src_ref=dst.at[q], dst_ref=dst.at[q], send_sem=ssem.at[d], recv_sem=rsem.at[d],
-                device_id=peer(d)[1], device_id_type=MESH,
-            ).wait_recv()
-
-    sent = to_group(lambda other: send.at[other], recv, a_s, a_r)
-    from_group(recv, a_s, a_r)
+    pl.semaphore_wait(barrier, len(in_group) + len(in_column))
+    spread(0, in_group, lambda other: send.at[other], recv, me)
+    whole(0, in_group, recv).wait_recv()
 
     cell = iota((BX * BY, 128), 1)
     place_xy = (iota((BX * BY, 128), 0) - (lax.shift_right_logical(cell, 5) * BY + (lax.shift_right_logical(cell, 3) & 3))).astype(F32)
@@ -272,8 +263,7 @@
         @pl.when(exists(*d))
         def _():
             halo(*d).start()
-    for c in sent:
-        c.wait_send()
+    whole(0, in_group, recv).wait_send()
     for d in order:
         @pl.when(exists(*d))
         def _():
@@ -332,32 +322,67 @@
         product = jnp.sum(basis[k // 2] * basis[(k + 1) // 2], axis=0)
         lines.append(jnp.sum(product, axis=0, keepdims=True))
     lines.append(jnp.zeros((2, 128), F32))
-    part[...] = jnp.concatenate(lines, 0)
-    parts[me] = part[...]
-    sent = to_group(lambda other: part, parts, g_s, g_r)
+    fold = jnp.concatenate(lines, 0)
+    for shift in (64, 32, 16):
+        fold = fold + pltpu.roll(fold, shift, 1)
+    own = lax.shift_right_logical(lane, 4) == sub
+
+    direct = nx * group <= 64
+    peers = everyone if direct else in_group
+    spot = gx * group + me if direct else me
+    line = jnp.sum(jnp.where(own, fold, 0.0), axis=0, keepdims=True)
+    part[...] = line
+    parts[spot] = line
+    spread(1, peers, lambda other: part, parts, spot)
+
+    flat = jnp.concatenate(halves(jnp.concatenate([v.reshape(BX * BY, BZ) for v in basis[:ITERS]], 0)), 0)
+    tall = ITERS * BX * BY
+
+    def gather(g, carry):
+        picked = lax.dot_general(flat, zhot[g], (((1,), (1,)), ((), ())), preferred_element_type=F32)
+        picked = picked[:tall] + picked[tall:]
+        got = recv[g]
+        at = [place_xy == got[3 * cap + k : 3 * cap + k + 1] for k in range(cap)]
+        lines = []
+        for v in range(ITERS):
+            for k in range(cap):
+                cells = picked[BX * BY * v : BX * BY * (v + 1), 128 * k : 128 * k + 128]
+                lines.append(jnp.sum(jnp.where(at[k], cells, 0.0), axis=0, keepdims=True))
+        lines.append(jnp.zeros((rows - ITERS * cap, 128), F32))
+        back[g] = jnp.concatenate(lines, 0)
+        return carry
+
+    repeat(group, gather, 0)
+    returned[me] = back[me]
+    spread(2, in_group, lambda other: back.at[other], returned, me)
     for d in order:
         @pl.when(exists(*d))
         def _():
             halo(*d).wait_send()
-    from_group(parts, g_s, g_r)
-    total = repeat(group, lambda g, t: t + parts[g], jnp.zeros((8, 128), F32))
-    colpart[...] = total
-    colparts[gx] = total
-    col = []
-    for d in range(1, nx):
-        c = pltpu.make_async_remote_copy(
-            src_ref=colpart, dst_ref=colparts.at[gx], send_sem=c_s.at[d], recv_sem=c_r.at[d],
-            device_id=(lax.rem(gx + d, nx), gy, gz), device_id_type=MESH,
-        )
-        c.start()
-        col.append(c)
-    for d in range(1, nx):
-        q = lax.rem(gx + nx - d, nx)
-        pltpu.make_async_remote_copy(
-            src_ref=colpart, dst_ref=colparts.at[q], send_sem=c_s.at[d], recv_sem=c_r.at[d],
-            device_id=(lax.rem(gx + d, nx), gy, gz), device_id_type=MESH,
-        ).wait_recv()
-    total = repeat(nx, lambda g, t: t + colparts[g], jnp.zeros((8, 128), F32))
+    tr = iota((slots, group * rows), 1)
+    inner = lax.rem(tr, rows)
+    want = (lax.div(tr, rows) * cap + lax.rem(inner, cap)).astype(F32)
+    sel = jnp.concatenate(
+        [jnp.where((lax.div(inner, cap) == v) & (want == tcol), 1.0, 0.0) for v in range(ITERS)], 0
+    )
+    whole(2, in_group, returned).wait_recv()
+    values = jnp.dot(sel, returned[...].reshape(group * rows, 128), precision=HI, preferred_element_type=F32)
+    left = jnp.concatenate(halves(values), 0)
+    for n in range(slots):
+        out = lax.dot_general(left, w_ref[n], (((1,), (1,)), ((), ())), preferred_element_type=F32)
+        for v in range(ITERS):
+            at = v * slots + n
+            values_at[v, n : n + 1, :] = out[at : at + 1] + out[ITERS * slots + at : ITERS * slots + at + 1]
+
+    whole(1, peers, parts).wait_recv()
+    total = repeat(len(peers) + 1, lambda g, t: t + parts[g], jnp.zeros((1, 128), F32))
+    if not direct:
+        colpart[...] = total
+        colparts[gx] = total
+        spread(3, in_column, lambda other: colpart, colparts, gx)
+        whole(3, in_column, colparts).wait_recv()
+        total = repeat(nx, lambda g, t: t + colparts[g], jnp.zeros((1, 128), F32))
+    total = jnp.where(own, jnp.broadcast_to(total, (8, 128)), 0.0)
     moments = jnp.broadcast_to(jnp.sum(total, axis=1, keepdims=True), (8, 128))
     field_c, resid_c = coefficients([moments[k : k + 1] for k in range(2 * ITERS)])
 
@@ -368,42 +393,17 @@
             out = term if out is None else out + term
         return out
 
-    field = combine(field_c)
-    field_ref[...] = field
-    flat = jnp.concatenate(halves(field.reshape(BX * BY, BZ)), 0)
-
-    def gather(g, carry):
-        picked = lax.dot_general(flat, zhot[g], (((1,), (1,)), ((), ())), preferred_element_type=F32)
-        picked = picked[: BX * BY] + picked[BX * BY :]
-        got = recv[g]
-        lines = []
-        for k in range(cap):
-            at = place_xy == got[3 * cap + k : 3 * cap + k + 1]
-            lines.append(
-                jnp.sum(jnp.where(at, picked[:, 128 * k : 128 * k + 128], 0.0), axis=0, keepdims=True)
-            )
-        lines.append(jnp.zeros((rows - cap, 128), F32))
-        back[g] = jnp.concatenate(lines, 0)
-        return carry
-
-    repeat(group, gather, 0)
-    returned[me] = back[me]
-    last = to_group(lambda other: back.at[other], returned, b_s, b_r)
+    field_ref[...] = combine(field_c)
     resid_ref[...] = combine(resid_c)
-    for c in sent + col:
-        c.wait_send()
-    tr = iota((slots, group * rows), 1)
-    inner = lax.rem(tr, rows)
-    want = (lax.div(tr, rows) * cap + inner).astype(F32)
-    sel = jnp.where((inner < cap) & (want == tcol), 1.0, 0.0)
-    from_group(returned, b_s, b_r)
-    values = jnp.dot(sel, returned[...].reshape(group * rows, 128), precision=HI, preferred_element_type=F32)
-    left = jnp.concatenate(halves(values), 0)
-    for n in range(slots):
-        out = lax.dot_general(left, w_ref[n], (((1,), (1,)), ((), ())), preferred_element_type=F32)
-        point_ref[n : n + 1, :] = out[n : n + 1] + out[slots + n : slots + n + 1]
-    for c in last:
-        c.wait_send()
+    point = None
+    for v, c in enumerate(field_c):
+        term = jnp.concatenate([c] * (values_at.shape[2] // 128), 1) * values_at[v]
+        point = term if point is None else point + term
+    point_ref[...] = point
+    whole(1, peers, parts).wait_send()
+    whole(2, in_group, returned).wait_send()
+    if not direct:
+        whole(3, in_column, colparts).wait_send()
 
 
 def shards(nx, ny, nz, spline_weights, point_source, confidence, block_dest, offsets, block_count):
@@ -420,7 +420,7 @@
             jax.ShapeDtypeStruct((BX, BY, BZ), F32),
             jax.ShapeDtypeStruct((slots, points), F32),
         ),
-        in_specs=[pl.BlockSpec(memory_space=pltpu.SMEM)] + [pl.BlockSpec(memory_space=pltpu.HBM)] * 5,
+        in_specs=[pl.BlockSpec(memory_space=pltpu.HBM)] * 5 + [pl.BlockSpec(memory_space=pltpu.SMEM)],
         out_specs=(vmem, vmem, vmem),
         scratch_shapes=[
             pltpu.VMEM((group, rows, 128), F32),
@@ -434,31 +434,32 @@
             pltpu.VMEM((2, BX // 2, 2, BY, BZ), F32),
             pltpu.VMEM((2, 2, 2, 2, BY, BZ), F32),
             pltpu.VMEM((2, 3, 2, BY, BZ), F32),
-            pltpu.VMEM((8, 128), F32),
-            pltpu.VMEM((group, 8, 128), F32),
-            pltpu.VMEM((8, 128), F32),
-            pltpu.VMEM((nx, 8, 128), F32),
+            pltpu.VMEM((1, 128), F32),
+            pltpu.VMEM((nx * group, 1, 128), F32),
+            pltpu.VMEM((1, 128), F32),
+            pltpu.VMEM((nx, 1, 128), F32),
             pltpu.VMEM((group, rows, 128), F32),
             pltpu.VMEM((group, rows, 128), F32),
             pltpu.VMEM((4 * slots, 128), F32),
+            pltpu.VMEM((ITERS, slots, points), F32),
             pltpu.VMEM(spline_weights.shape, BF16),
             pltpu.VMEM(point_source.shape, F32),
             pltpu.VMEM(confidence.shape, F32),
             pltpu.VMEM((1, slots), jnp.int32),
             pltpu.VMEM(offsets.shape, jnp.int32),
-            dma((5,)),
-            dma((group,)), dma((group,)), dma((27,)), dma((27,)), dma((group,)), dma((group,)),
-            dma((nx,)), dma((nx,)), dma((group,)), dma((group,)),
+            dma((6,)), dma((27,)), dma((27,)), dma((4,)), dma((4,)),
         ],
         compiler_params=pltpu.CompilerParams(
             collective_id=0, has_side_effects=True, vmem_limit_bytes=40 * 1024 * 1024
         ),
     )(
-        block_count,
         *(
             pltpu.with_memory_space_constraint(a, pltpu.HBM)
-            for a in (spline_weights, point_source, confidence, block_dest.reshape(1, slots), offsets)
+            for a in (
+                spline_weights, point_source, confidence, block_dest.reshape(1, slots), offsets,
+            )
         ),
+        block_count.reshape((1,)),
     )
 
 

time: 30 us -> 23.6 us (0.79)
  Pallas kernels: 26.7 us -> 20.3 us
    pallas_call x1, Pallas kernels: 26.7 us -> 20.3 us  [shards(): pl.pallas_call(functools.partial(kernel, (nx, ny, nz, slots, cap)), out_s...]
where the time goes in v1:
time: 23.6 us; the launch traced here: 23.4 us
  Pallas kernels  20.3 us (86%)
  local copies, waits for them, and re-layouts  1.83 us (8%)
  between operations  1.29 us (5%)
    pallas_call x1, Pallas kernels, shards(): pl.pallas_call(functools.partial(kernel, (nx, ny, nz, slots, cap)), out_s...  20.3 us
    unnamed x3, local copies, waits for them, and re-layouts  1.83 us

profile of v1, /device:TPU:0, one launch (start us, length us, event | category | flops | bytes accessed | tf_op | source)
XLA Modules:
  0.0 23.4 jit_solution(20353742878309875)
XLA Ops:
  1.3 20.3 %shard_map.85 = (f32[8,8,128]{2,1,0:T(8,128)S(1)}, f32[8,8,128]{2,1,0:T(8,128)S(1)}, f32[8,256]{1,0:T(8,128)S(1)}) custom-call(bf16[8,256,128]{2,1,0:T(8,128)(2,1)} %w_hbm.1, f32[8,256]{1,0:T(8,128)} %src_hbm.1, f32[8,256]{1,0:T(8,128)} %conf_hbm.1, s32[1,8]{1,0:T(1,128)} %bitcast.1, s32[3,8]{1,0:T(4,128)} %off_hbm.1, s32[1]{0:T(128)S(6)} %copy.12.count_hbm), custom_call_target="tpu_custom_call" | custom-call | tf_op jit(solution)/shard_map/pallas_call | solution.py:416
  21.6 0.6 %copy.13 = f32[8,8,128]{2,1,0:T(8,128)} copy(f32[8,8,128]{2,1,0:T(8,128)S(1)} %get-tuple-element.6) | data formatting | bytes 65536
  22.2 0.6 %copy.14 = f32[8,8,128]{2,1,0:T(8,128)} copy(f32[8,8,128]{2,1,0:T(8,128)S(1)} %get-tuple-element.7) | data formatting | bytes 65536
  22.8 0.6 %copy.15 = f32[8,256]{1,0:T(8,128)} copy(f32[8,256]{1,0:T(8,128)S(1)} %get-tuple-element.8) | data formatting | bytes 16384

commit v2 on v1

--- a/solution.py
+++ b/solution.py
@@ -88,9 +88,9 @@
 
 
 def kernel(sizes, w_hbm, src_hbm, conf_hbm, dest_hbm, off_hbm, count_hbm,
-           field_ref, resid_ref, point_ref,
+           basis_ref, values_at, sums_ref,
            send, recv, zhot, fbuf, ylow, yhigh, zpack, zrecv, yrecv, erecv, xrecv,
-           part, parts, colpart, colparts, back, returned, pay, values_at,
+           part, parts, colpart, colparts, back, returned, pay,
            w_ref, src_ref, conf_ref, dest_ref, off_ref, in_s, h_s, h_r, one_s, one_r):
     nx, ny, nz, slots, cap = sizes
     group = ny * nz
@@ -139,6 +139,9 @@
             )
         )
     ]
+    barrier = pltpu.get_barrier_semaphore()
+    for _, where in reversed(in_group):
+        pl.semaphore_signal(barrier, inc=1, device_id=where, device_id_type=MESH)
     for c in loads:
         c.start()
     zrecv[...] = jnp.zeros_like(zrecv)
@@ -146,8 +149,7 @@
     erecv[...] = jnp.zeros_like(erecv)
     xrecv[...] = jnp.zeros_like(xrecv)
 
-    barrier = pltpu.get_barrier_semaphore()
-    for _, where in in_group + in_column:
+    for _, where in in_column:
         pl.semaphore_signal(barrier, inc=1, device_id=where, device_id_type=MESH)
 
     for c in loads[:2]:
@@ -317,6 +319,7 @@
     v2 = step(v1, 2)
     v3 = step(v2, 3)
     basis = [rhs, v1[2:10, :8, :128], v2[1:9, :8, :128], v3[:, :8, :128]]
+    basis_ref[0] = rhs
     lines = []
     for k in range(2 * ITERS):
         product = jnp.sum(basis[k // 2] * basis[(k + 1) // 2], axis=0)
@@ -334,6 +337,8 @@
     part[...] = line
     parts[spot] = line
     spread(1, peers, lambda other: part, parts, spot)
+    for k in range(1, ITERS + 1):
+        basis_ref[k] = basis[k]
 
     flat = jnp.concatenate(halves(jnp.concatenate([v.reshape(BX * BY, BZ) for v in basis[:ITERS]], 0)), 0)
     tall = ITERS * BX * BY
@@ -382,28 +387,40 @@
         spread(3, in_column, lambda other: colpart, colparts, gx)
         whole(3, in_column, colparts).wait_recv()
         total = repeat(nx, lambda g, t: t + colparts[g], jnp.zeros((1, 128), F32))
-    total = jnp.where(own, jnp.broadcast_to(total, (8, 128)), 0.0)
-    moments = jnp.broadcast_to(jnp.sum(total, axis=1, keepdims=True), (8, 128))
+    sums_ref[...] = jnp.where(own, jnp.broadcast_to(total, (8, 128)), 0.0)
+    whole(1, peers, parts).wait_send()
+    whole(2, in_group, returned).wait_send()
+    if not direct:
+        whole(3, in_column, colparts).wait_send()
+
+
+def finish(basis_ref, values_at, sums_ref, field_hbm, resid_hbm, point_hbm, field_ref, resid_ref, point_ref, out_s):
+    moments = jnp.broadcast_to(jnp.sum(sums_ref[...], axis=1, keepdims=True), (8, 128))
     field_c, resid_c = coefficients([moments[k : k + 1] for k in range(2 * ITERS)])
+    copies = [
+        pltpu.make_async_copy(a, b, out_s.at[i])
+        for i, (a, b) in enumerate(((field_ref, field_hbm), (point_ref, point_hbm), (resid_ref, resid_hbm)))
+    ]
 
     def combine(cs):
         out = None
-        for c, v in zip(cs, basis):
-            term = c.reshape(1, 1, 128) * v
+        for k, c in enumerate(cs):
+            term = c.reshape(1, 1, 128) * basis_ref[k]
             out = term if out is None else out + term
         return out
 
     field_ref[...] = combine(field_c)
-    resid_ref[...] = combine(resid_c)
+    copies[0].start()
     point = None
     for v, c in enumerate(field_c):
         term = jnp.concatenate([c] * (values_at.shape[2] // 128), 1) * values_at[v]
         point = term if point is None else point + term
     point_ref[...] = point
-    whole(1, peers, parts).wait_send()
-    whole(2, in_group, returned).wait_send()
-    if not direct:
-        whole(3, in_column, colparts).wait_send()
+    copies[1].start()
+    resid_ref[...] = combine(resid_c)
+    copies[2].start()
+    for c in copies:
+        c.wait()
 
 
 def shards(nx, ny, nz, spline_weights, point_source, confidence, block_dest, offsets, block_count):
@@ -413,14 +430,16 @@
     rows = 4 * cap
     vmem = pl.BlockSpec(memory_space=pltpu.VMEM)
     dma = pltpu.SemaphoreType.DMA
-    return pl.pallas_call(
+    hbm = pl.BlockSpec(memory_space=pltpu.HBM)
+    brick = jax.ShapeDtypeStruct((BX, BY, BZ), F32)
+    middle = pl.pallas_call(
         functools.partial(kernel, (nx, ny, nz, slots, cap)),
         out_shape=(
-            jax.ShapeDtypeStruct((BX, BY, BZ), F32),
-            jax.ShapeDtypeStruct((BX, BY, BZ), F32),
-            jax.ShapeDtypeStruct((slots, points), F32),
+            jax.ShapeDtypeStruct((ITERS + 1, BX, BY, BZ), F32),
+            jax.ShapeDtypeStruct((ITERS, slots, points), F32),
+            jax.ShapeDtypeStruct((8, 128), F32),
         ),
-        in_specs=[pl.BlockSpec(memory_space=pltpu.HBM)] * 5 + [pl.BlockSpec(memory_space=pltpu.SMEM)],
+        in_specs=[hbm] * 5 + [pl.BlockSpec(memory_space=pltpu.SMEM)],
         out_specs=(vmem, vmem, vmem),
         scratch_shapes=[
             pltpu.VMEM((group, rows, 128), F32),
@@ -441,7 +460,6 @@
             pltpu.VMEM((group, rows, 128), F32),
             pltpu.VMEM((group, rows, 128), F32),
             pltpu.VMEM((4 * slots, 128), F32),
-            pltpu.VMEM((ITERS, slots, points), F32),
             pltpu.VMEM(spline_weights.shape, BF16),
             pltpu.VMEM(point_source.shape, F32),
             pltpu.VMEM(confidence.shape, F32),
@@ -461,6 +479,19 @@
         ),
         block_count.reshape((1,)),
     )
+    return pl.pallas_call(
+        finish,
+        out_shape=(brick, brick, jax.ShapeDtypeStruct((slots, points), F32)),
+        in_specs=[vmem] * 3,
+        out_specs=(hbm, hbm, hbm),
+        scratch_shapes=[
+            pltpu.VMEM((BX, BY, BZ), F32),
+            pltpu.VMEM((BX, BY, BZ), F32),
+            pltpu.VMEM((slots, points), F32),
+            dma((3,)),
+        ],
+        compiler_params=pltpu.CompilerParams(vmem_limit_bytes=4 * 1024 * 1024),
+    )(*middle)
 
 
 def solution(mesh):

time: 23.6 us -> 22.4 us (0.949)
  local copies, waits for them, and re-layouts: 1.83 us -> 0 us
  Pallas kernels: 20.3 us -> 21 us
    unnamed x3 -> x0, local copies, waits for them, and re-layouts: 1.83 us -> none
    pallas_call x0 -> x1, Pallas kernels: none -> 0.82 us  [shards(): pl.pallas_call(finish, out_shape=(brick, brick, jax.ShapeDtypeStruct((slo...]
where the time goes in v2:
time: 22.4 us; the launch traced here: 22.3 us
  Pallas kernels  21 us (94%)
  between operations  1.29 us (6%)
    pallas_call x1, Pallas kernels, shards(): pl.pallas_call(functools.partial(kernel, (nx, ny, nz, slots, cap)), out_s...  20.2 us
    pallas_call x1, Pallas kernels, shards(): pl.pallas_call(finish, out_shape=(brick, brick, jax.ShapeDtypeStruct((slo...  0.82 us

profile of v2, /device:TPU:0, one launch (start us, length us, event | category | flops | bytes accessed | tf_op | source)
XLA Modules:
  0.0 22.3 jit_solution(12457464843731949780)
XLA Ops:
  1.3 20.2 %shard_map.85 = (f32[4,8,8,128]{3,2,1,0:T(8,128)S(1)}, f32[3,8,256]{2,1,0:T(8,128)S(1)}, f32[8,128]{1,0:T(8,128)S(1)}) custom-call(bf16[8,256,128]{2,1,0:T(8,128)(2,1)} %w_hbm.1, f32[8,256]{1,0:T(8,128)} %src_hbm.1, f32[8,256]{1,0:T(8,128)} %conf_hbm.1, s32[1,8]{1,0:T(1,128)} %bitcast.1, s32[3,8]{1,0:T(4,128)} %off_hbm.1, s32[1]{0:T(128)S(6)} %copy.9.count_hbm), custom_call_target="tpu_custom_call" | custom-call | tf_op jit(solution)/shard_map/pallas_call | solution.py:435
  21.5 0.8 %shard_map.86 = (f32[8,8,128]{2,1,0:T(8,128)}, f32[8,8,128]{2,1,0:T(8,128)}, f32[8,256]{1,0:T(8,128)}) custom-call(f32[4,8,8,128]{3,2,1,0:T(8,128)S(1)} %get-tuple-element.6.basis_ref, f32[3,8,256]{2,1,0:T(8,128)S(1)} %get-tuple-element.7.values_at, f32[8,128]{1,0:T(8,128)S(1)} %get-tuple-element.8.sums_ref), custom_call_target="tpu_custom_call" | custom-call | tf_op jit(solution)/shard_map/pallas_call | solution.py:482

commit v3 on v2

--- a/solution.py
+++ b/solution.py
@@ -26,6 +26,11 @@
 ]
 
 
+YAT = 27
+XYAT = YAT + 12
+XAT = XYAT + 12
+
+
 def code(dx, dy, dz):
     return (dx + 1) * 9 + (dy + 1) * 3 + (dz + 1)
 
@@ -89,9 +94,9 @@
 
 def kernel(sizes, w_hbm, src_hbm, conf_hbm, dest_hbm, off_hbm, count_hbm,
            basis_ref, values_at, sums_ref,
-           send, recv, zhot, fbuf, ylow, yhigh, zpack, zrecv, yrecv, erecv, xrecv,
+           send, recv, zhot, xlow, xhigh, ylow, yhigh, zpack, halo_in,
            part, parts, colpart, colparts, back, returned, pay,
-           w_ref, src_ref, conf_ref, dest_ref, off_ref, in_s, h_s, h_r, one_s, one_r):
+           w_ref, src_ref, conf_ref, dest_ref, off_ref, in_s, one_s, one_r):
     nx, ny, nz, slots, cap = sizes
     group = ny * nz
     gx, gy, gz = lax.axis_index("gx"), lax.axis_index("gy"), lax.axis_index("gz")
@@ -144,10 +149,8 @@
         pl.semaphore_signal(barrier, inc=1, device_id=where, device_id_type=MESH)
     for c in loads:
         c.start()
-    zrecv[...] = jnp.zeros_like(zrecv)
-    yrecv[...] = jnp.zeros_like(yrecv)
-    erecv[...] = jnp.zeros_like(erecv)
-    xrecv[...] = jnp.zeros_like(xrecv)
+    back[...] = jnp.zeros_like(back)
+    halo_in[...] = jnp.zeros_like(halo_in)
 
     for _, where in in_column:
         pl.semaphore_signal(barrier, inc=1, device_id=where, device_id_type=MESH)
@@ -220,6 +223,25 @@
         zhot[g] = hot
         return acc + jnp.dot(jnp.concatenate(lefts, 1), hot, preferred_element_type=F32)
 
+    def gather_of(vectors, first):
+        flat = jnp.concatenate(halves(jnp.concatenate([v.reshape(BX * BY, BZ) for v in vectors], 0)), 0)
+        tall = flat.shape[0] // 2
+
+        def gather(g, carry):
+            picked = lax.dot_general(flat, zhot[g], (((1,), (1,)), ((), ())), preferred_element_type=F32)
+            picked = picked[:tall] + picked[tall:]
+            got = recv[g]
+            at = [place_xy == got[3 * cap + k : 3 * cap + k + 1] for k in range(cap)]
+            lines = []
+            for v in range(len(vectors)):
+                for k in range(cap):
+                    cells = picked[BX * BY * v : BX * BY * (v + 1), 128 * k : 128 * k + 128]
+                    lines.append(jnp.sum(jnp.where(at[k], cells, 0.0), axis=0, keepdims=True))
+            back[g, first * cap : (first + len(vectors)) * cap, :] = jnp.concatenate(lines, 0)
+            return carry
+
+        repeat(group, gather, 0)
+
     acc = repeat(group, scatter, jnp.zeros((4 * BX * BY, BZ), F32))
     both = acc[: 2 * BX * BY] + acc[2 * BX * BY :]
     rhs = both[: BX * BY].reshape(BX, BY, BZ)
@@ -228,68 +250,113 @@
     lane = iota((BY, BZ), 1)
     sub = iota((BY, BZ), 0)
     rim = (lane < 3) | (lane >= BZ - 3)
+    for half in range(2):
+        for q in range(2):
+            j = 2 * half + q
+            even, odd = rhs[2 * j], pltpu.roll(rhs[2 * j + 1], 4, 0)
+            ylow[3 * half + q] = jnp.where(sub < 4, even, odd)
+            yhigh[3 * half + q] = jnp.where(sub < 4, odd, even)
+        low, high = den[4 * half], pltpu.roll(den[4 * half], 2, 0)
+        for p in range(1, 4):
+            pick = lax.shift_right_logical(sub, 1) == p
+            plane = den[4 * half + p]
+            low = jnp.where(pick, pltpu.roll(plane, 2 * p, 0), low)
+            high = jnp.where(pick, pltpu.roll(plane, (2 * p + 2) % 8, 0) if p < 3 else plane, high)
+        ylow[3 * half + 2] = low
+        yhigh[3 * half + 2] = high
+
+    def buffers(dx, dy, dz):
+        if dz:
+            return zpack, halo_in.at[code(-dx, -dy, -dz)]
+        if dy:
+            source = ylow if dy < 0 else yhigh
+            side = 0 if dy > 0 else 1
+            if not dx:
+                return source, halo_in.at[pl.ds(YAT + 6 * side, 6)]
+            at = XYAT + 3 * (side if dx > 0 else 2 + side)
+            return source.at[pl.ds(3 if dx > 0 else 0, 3)], halo_in.at[pl.ds(at, 3)]
+        return xhigh if dx > 0 else xlow, halo_in.at[pl.ds(XAT if dx > 0 else XAT + 5, 5)]
+
+    def halo(dx, dy, dz):
+        source, target = buffers(dx, dy, dz)
+        return pltpu.make_async_remote_copy(
+            src_ref=source, dst_ref=target,
+            send_sem=one_s.at[4], recv_sem=one_r.at[4],
+            device_id=(gx + dx, gy + dy, gz + dz), device_id_type=MESH,
+        )
+
+    order = sorted(DIRS, key=lambda d: (d[2] != 0, d[1] == 0, d[0] != 0))
+
+    def depart(directions):
+        for d in directions:
+            @pl.when(exists(*d))
+            def _():
+                halo(*d).start()
+
+    depart([d for d in order if d[1] and not d[2]])
+    for i in range(3):
+        xlow[i], xhigh[i] = rhs[i], rhs[5 + i]
+    for i in range(2):
+        xlow[3 + i], xhigh[3 + i] = den[i], den[6 + i]
     packed = jnp.zeros((BY, BZ), F32)
     for f, field in enumerate((rhs, den)):
         for x in range(BX):
             edge = jnp.where(rim, field[x], 0.0)
             shift = 8 * x + 64 * f
             packed = packed + (pltpu.roll(edge, shift, 1) if shift else edge)
-            fbuf[x, f] = field[x]
-        for j in range(BX // 2):
-            even, odd = field[2 * j], pltpu.roll(field[2 * j + 1], 4, 0)
-            ylow[j, f] = jnp.where(sub < 4, even, odd)
-            yhigh[j, f] = jnp.where(sub < 4, odd, even)
     zpack[...] = packed
-
-    def buffers(dx, dy, dz):
-        if dz:
-            return zpack, zrecv.at[code(-dx, -dy, -dz)]
-        if dy:
-            source = ylow if dy < 0 else yhigh
-            side = 0 if dy > 0 else 1
-            if not dx:
-                return source, yrecv.at[side]
-            return source.at[pl.ds(2 if dx > 0 else 0, 2)], erecv.at[0 if dx > 0 else 1, side]
-        return fbuf.at[pl.ds(5 if dx > 0 else 0, 3)], xrecv.at[0 if dx > 0 else 1]
-
-    def halo(dx, dy, dz):
-        source, target = buffers(dx, dy, dz)
-        return pltpu.make_async_remote_copy(
-            src_ref=source, dst_ref=target,
-            send_sem=h_s.at[code(dx, dy, dz)], recv_sem=h_r.at[code(-dx, -dy, -dz)],
-            device_id=(gx + dx, gy + dy, gz + dz), device_id_type=MESH,
-        )
-
-    order = sorted(DIRS, key=lambda d: (d[2] != 0, d[0] != 0))
-    for d in order:
-        @pl.when(exists(*d))
-        def _():
-            halo(*d).start()
+    depart([d for d in order if d[2] or not d[1]])
+    basis_ref[0] = rhs
+    gather_of((rhs,), 0)
     whole(0, in_group, recv).wait_send()
-    for d in order:
-        @pl.when(exists(*d))
-        def _():
-            dx, dy, dz = d
-            halo(-dx, -dy, -dz).wait_recv()
+    near = [jnp.minimum(g, 1) + jnp.minimum(n - 1 - g, 1) for g, n in ((gx, nx), (gy, ny), (gz, nz))]
+    usual = [(0,) if n == 1 else (1,) if n == 2 else (1, 2) for n in (nx, ny, nz)]
+
+    def all_halos(finish_one):
+        for a in usual[0]:
+            for b in usual[1]:
+                for c in usual[2]:
+                    tiles = 5 * a + 6 * b + 3 * a * b + c * (1 + a) * (1 + b)
+                    if tiles:
+                        @pl.when((near[0] == a) & (near[1] == b) & (near[2] == c))
+                        def _():
+                            ref = halo_in.at[pl.ds(0, tiles)]
+                            finish_one(
+                                pltpu.make_async_remote_copy(
+                                    src_ref=ref, dst_ref=ref, send_sem=one_s.at[4], recv_sem=one_r.at[4],
+                                    device_id=(gx, gy, gz), device_id_type=MESH,
+                                )
+                            )
+
+    all_halos(lambda c: c.wait_recv())
 
     def rim_pack(dx, dy):
-        return jnp.where((lane & 7) < 4, zrecv[code(dx, dy, 1)], zrecv[code(dx, dy, -1)])
+        return jnp.where((lane & 7) < 4, halo_in[code(dx, dy, 1)], halo_in[code(dx, dy, -1)])
 
     fields = [[], []]
-    for dx, xs in ((-1, (5, 6, 7)), (0, tuple(range(BX))), (1, (0, 1, 2))):
+    none = jnp.zeros((2 * BY, 2 * BZ), F32)
+    for dx, xs_of in ((-1, (5, 6, 7)), (0, tuple(range(BX))), (1, (0, 1, 2))):
         pack0 = rim_pack(dx, 0)
         pack1 = jnp.where(sub < 4, rim_pack(dx, 1), rim_pack(dx, -1))
-        for i, x in enumerate(xs):
+        for i, x in enumerate(xs_of):
             for f in range(2):
+                if f and x == (5 if dx < 0 else 2 if dx > 0 else -1):
+                    fields[f].append(none)
+                    continue
+                half, p = x // 4, x % 4
+                at = (3 * half if dx == 0 else 0) + (2 if f else p // 2)
                 if dx:
                     side = 0 if dx < 0 else 1
-                    own = xrecv[side, i, f]
-                    pair = x // 2 - (2 if dx < 0 else 0)
-                    low, high = erecv[side, 1, pair, f], erecv[side, 0, pair, f]
+                    own = halo_in[XAT + 5 * side + (3 + (x % 6) if f else i)]
+                    low, high = (halo_in[XYAT + 3 * (2 * side + v) + at] for v in (1, 0))
                 else:
-                    own = fbuf[x, f]
-                    low, high = yrecv[1, x // 2, f], yrecv[0, x // 2, f]
-                if x % 2 == 0:
+                    own = (rhs, den)[f][x]
+                    low, high = halo_in[YAT + 6 + at], halo_in[YAT + at]
+                if f:
+                    low = pltpu.roll(low, 8 - 2 * p, 0) if p else low
+                    high = pltpu.roll(high, 6 - 2 * p, 0) if p < 3 else high
+                    beside = jnp.where(sub < 4, low, high)
+                elif x % 2 == 0:
                     beside = jnp.where(sub < 4, low, high)
                 else:
                     beside = pltpu.roll(jnp.where(sub < 4, high, low), 4, 0)
@@ -319,7 +386,6 @@
     v2 = step(v1, 2)
     v3 = step(v2, 3)
     basis = [rhs, v1[2:10, :8, :128], v2[1:9, :8, :128], v3[:, :8, :128]]
-    basis_ref[0] = rhs
     lines = []
     for k in range(2 * ITERS):
         product = jnp.sum(basis[k // 2] * basis[(k + 1) // 2], axis=0)
@@ -340,39 +406,24 @@
     for k in range(1, ITERS + 1):
         basis_ref[k] = basis[k]
 
-    flat = jnp.concatenate(halves(jnp.concatenate([v.reshape(BX * BY, BZ) for v in basis[:ITERS]], 0)), 0)
-    tall = ITERS * BX * BY
-
-    def gather(g, carry):
-        picked = lax.dot_general(flat, zhot[g], (((1,), (1,)), ((), ())), preferred_element_type=F32)
-        picked = picked[:tall] + picked[tall:]
-        got = recv[g]
-        at = [place_xy == got[3 * cap + k : 3 * cap + k + 1] for k in range(cap)]
-        lines = []
-        for v in range(ITERS):
-            for k in range(cap):
-                cells = picked[BX * BY * v : BX * BY * (v + 1), 128 * k : 128 * k + 128]
-                lines.append(jnp.sum(jnp.where(at[k], cells, 0.0), axis=0, keepdims=True))
-        lines.append(jnp.zeros((rows - ITERS * cap, 128), F32))
-        back[g] = jnp.concatenate(lines, 0)
-        return carry
-
-    repeat(group, gather, 0)
+    gather_of(basis[1:ITERS], 1)
     returned[me] = back[me]
     spread(2, in_group, lambda other: back.at[other], returned, me)
-    for d in order:
-        @pl.when(exists(*d))
-        def _():
-            halo(*d).wait_send()
+    all_halos(lambda c: c.wait_send())
     tr = iota((slots, group * rows), 1)
     inner = lax.rem(tr, rows)
     want = (lax.div(tr, rows) * cap + lax.rem(inner, cap)).astype(F32)
     sel = jnp.concatenate(
         [jnp.where((lax.div(inner, cap) == v) & (want == tcol), 1.0, 0.0) for v in range(ITERS)], 0
+    ).astype(BF16)
+    whole(2, in_group, returned).wait_recv()
+    left = jnp.concatenate(
+        [
+            jnp.dot(sel, part_of, preferred_element_type=F32).astype(BF16)
+            for part_of in halves(returned[...].reshape(group * rows, 128))
+        ],
+        0,
     )
-    whole(2, in_group, returned).wait_recv()
-    values = jnp.dot(sel, returned[...].reshape(group * rows, 128), precision=HI, preferred_element_type=F32)
-    left = jnp.concatenate(halves(values), 0)
     for n in range(slots):
         out = lax.dot_general(left, w_ref[n], (((1,), (1,)), ((), ())), preferred_element_type=F32)
         for v in range(ITERS):
@@ -380,13 +431,13 @@
             values_at[v, n : n + 1, :] = out[at : at + 1] + out[ITERS * slots + at : ITERS * slots + at + 1]
 
     whole(1, peers, parts).wait_recv()
-    total = repeat(len(peers) + 1, lambda g, t: t + parts[g], jnp.zeros((1, 128), F32))
+    total = jnp.sum(parts[pl.ds(0, len(peers) + 1)], axis=0)
     if not direct:
         colpart[...] = total
         colparts[gx] = total
         spread(3, in_column, lambda other: colpart, colparts, gx)
         whole(3, in_column, colparts).wait_recv()
-        total = repeat(nx, lambda g, t: t + colparts[g], jnp.zeros((1, 128), F32))
+        total = jnp.sum(colparts[...], axis=0)
     sums_ref[...] = jnp.where(own, jnp.broadcast_to(total, (8, 128)), 0.0)
     whole(1, peers, parts).wait_send()
     whole(2, in_group, returned).wait_send()
@@ -445,14 +496,12 @@
             pltpu.VMEM((group, rows, 128), F32),
             pltpu.VMEM((group, rows, 128), F32),
             pltpu.VMEM((group, cap * 128, BZ), BF16),
-            pltpu.VMEM((BX, 2, BY, BZ), F32),
-            pltpu.VMEM((BX // 2, 2, BY, BZ), F32),
-            pltpu.VMEM((BX // 2, 2, BY, BZ), F32),
+            pltpu.VMEM((5, BY, BZ), F32),
+            pltpu.VMEM((5, BY, BZ), F32),
+            pltpu.VMEM((6, BY, BZ), F32),
+            pltpu.VMEM((6, BY, BZ), F32),
             pltpu.VMEM((BY, BZ), F32),
-            pltpu.VMEM((27, BY, BZ), F32),
-            pltpu.VMEM((2, BX // 2, 2, BY, BZ), F32),
-            pltpu.VMEM((2, 2, 2, 2, BY, BZ), F32),
-            pltpu.VMEM((2, 3, 2, BY, BZ), F32),
+            pltpu.VMEM((XAT + 10, BY, BZ), F32),
             pltpu.VMEM((1, 128), F32),
             pltpu.VMEM((nx * group, 1, 128), F32),
             pltpu.VMEM((1, 128), F32),
@@ -465,7 +514,7 @@
             pltpu.VMEM(confidence.shape, F32),
             pltpu.VMEM((1, slots), jnp.int32),
             pltpu.VMEM(offsets.shape, jnp.int32),
-            dma((6,)), dma((27,)), dma((27,)), dma((4,)), dma((4,)),
+            dma((6,)), dma((5,)), dma((5,)),
         ],
         compiler_params=pltpu.CompilerParams(
             collective_id=0, has_side_effects=True, vmem_limit_bytes=40 * 1024 * 1024

time: 22.4 us -> 21.5 us (0.960)
  Pallas kernels: 21 us -> 20 us
    pallas_call x1, Pallas kernels: 20.2 us -> 19.2 us  [shards(): pl.pallas_call(functools.partial(kernel, (nx, ny, nz, slots, cap)), out_s...]
where the time goes in v3:
time: 21.5 us; the launch traced here: 21.3 us
  Pallas kernels  20 us (93%)
  between operations  1.29 us (6%)
    pallas_call x1, Pallas kernels, shards(): pl.pallas_call(functools.partial(kernel, (nx, ny, nz, slots, cap)), out_s...  19.2 us
    pallas_call x1, Pallas kernels, shards(): pl.pallas_call(finish, out_shape=(brick, brick, jax.ShapeDtypeStruct((slo...  0.82 us

profile of v3, /device:TPU:0, one launch (start us, length us, event | category | flops | bytes accessed | tf_op | source)
XLA Modules:
  0.0 21.3 jit_solution(8391774600871588409)
XLA Ops:
  1.3 19.2 %shard_map.85 = (f32[4,8,8,128]{3,2,1,0:T(8,128)S(1)}, f32[3,8,256]{2,1,0:T(8,128)S(1)}, f32[8,128]{1,0:T(8,128)S(1)}) custom-call(bf16[8,256,128]{2,1,0:T(8,128)(2,1)} %w_hbm.1, f32[8,256]{1,0:T(8,128)} %src_hbm.1, f32[8,256]{1,0:T(8,128)} %conf_hbm.1, s32[1,8]{1,0:T(1,128)} %bitcast.1, s32[3,8]{1,0:T(4,128)} %off_hbm.1, s32[1]{0:T(128)S(6)} %copy.9.count_hbm), custom_call_target="tpu_custom_call" | custom-call | tf_op jit(solution)/shard_map/pallas_call | solution.py:486
  20.5 0.8 %shard_map.86 = (f32[8,8,128]{2,1,0:T(8,128)}, f32[8,8,128]{2,1,0:T(8,128)}, f32[8,256]{1,0:T(8,128)}) custom-call(f32[4,8,8,128]{3,2,1,0:T(8,128)S(1)} %get-tuple-element.6.basis_ref, f32[3,8,256]{2,1,0:T(8,128)S(1)} %get-tuple-element.7.values_at, f32[8,128]{1,0:T(8,128)S(1)} %get-tuple-element.8.sums_ref), custom_call_target="tpu_custom_call" | custom-call | tf_op jit(solution)/shard_map/pallas_call | solution.py:531

commit v4 on v3

--- a/solution.py
+++ b/solution.py
@@ -107,6 +107,8 @@
 
     xs, ys, zs = ring(gx, nx), ring(gy, ny), ring(gz, nz)
     in_group = [(y * nz + z, (gx, y, z)) for y in ys for z in zs][1:]
+    nearby = [(ys[y] * nz + zs[z], (gx, ys[y], zs[z])) for y in range(ny) for z in range(0, nz, 2)][1:]
+    beyond = [(ys[y] * nz + zs[z], (gx, ys[y], zs[z])) for y in range(ny) for z in range(1, nz, 2)]
     in_column = [(x, (x, gy, gz)) for x in xs][1:]
     everyone = [((x * ny + y) * nz + z, (x, y, z)) for x in xs for y in ys for z in zs][1:]
 
@@ -201,8 +203,8 @@
     recv[me] = send[me]
 
     pl.semaphore_wait(barrier, len(in_group) + len(in_column))
-    spread(0, in_group, lambda other: send.at[other], recv, me)
-    whole(0, in_group, recv).wait_recv()
+    spread(0, nearby, lambda other: send.at[other], recv, me)
+    spread(5, beyond, lambda other: send.at[other], recv, me)
 
     cell = iota((BX * BY, 128), 1)
     place_xy = (iota((BX * BY, 128), 0) - (lax.shift_right_logical(cell, 5) * BY + (lax.shift_right_logical(cell, 3) & 3))).astype(F32)
@@ -242,7 +244,19 @@
 
         repeat(group, gather, 0)
 
-    acc = repeat(group, scatter, jnp.zeros((4 * BX * BY, BZ), F32))
+    acc = jnp.zeros((4 * BX * BY, BZ), F32)
+    if group <= 8:
+        back_y, back_z = ([lax.rem(g + n - d, n) for d in range(n)] for g, n in ((gy, ny), (gz, nz)))
+        for first, kind, peers_of in ((0, 0, nearby), (1, 5, beyond)):
+            if peers_of:
+                whole(kind, peers_of, recv).wait_recv()
+            for y in range(ny):
+                for z in range(first, nz, 2):
+                    acc = scatter(back_y[y] * nz + back_z[z], acc)
+    else:
+        whole(0, nearby, recv).wait_recv()
+        whole(5, beyond, recv).wait_recv()
+        acc = repeat(group, scatter, acc)
     both = acc[: 2 * BX * BY] + acc[2 * BX * BY :]
     rhs = both[: BX * BY].reshape(BX, BY, BZ)
     den = (0.25 * both[BX * BY :]).reshape(BX, BY, BZ)
@@ -308,7 +322,8 @@
     depart([d for d in order if d[2] or not d[1]])
     basis_ref[0] = rhs
     gather_of((rhs,), 0)
-    whole(0, in_group, recv).wait_send()
+    whole(0, nearby, recv).wait_send()
+    whole(5, beyond, recv).wait_send()
     near = [jnp.minimum(g, 1) + jnp.minimum(n - 1 - g, 1) for g, n in ((gx, nx), (gy, ny), (gz, nz))]
     usual = [(0,) if n == 1 else (1,) if n == 2 else (1, 2) for n in (nx, ny, nz)]
 
@@ -514,7 +529,7 @@
             pltpu.VMEM(confidence.shape, F32),
             pltpu.VMEM((1, slots), jnp.int32),
             pltpu.VMEM(offsets.shape, jnp.int32),
-            dma((6,)), dma((5,)), dma((5,)),
+            dma((6,)), dma((6,)), dma((6,)),
         ],
         compiler_params=pltpu.CompilerParams(
             collective_id=0, has_side_effects=True, vmem_limit_bytes=40 * 1024 * 1024

time: 21.5 us -> 21.3 us (level)
  no operation moved by 1% of the time
where the time goes in v4:
time: 21.3 us; the launch traced here: 21.2 us
  Pallas kernels  19.9 us (93%)
  between operations  1.29 us (6%)
    pallas_call x1, Pallas kernels, shards(): pl.pallas_call(functools.partial(kernel, (nx, ny, nz, slots, cap)), out_s...  19.1 us
    pallas_call x1, Pallas kernels, shards(): pl.pallas_call(finish, out_shape=(brick, brick, jax.ShapeDtypeStruct((slo...  0.82 us

profile of v4, /device:TPU:0, one launch (start us, length us, event | category | flops | bytes accessed | tf_op | source)
XLA Modules:
  0.0 21.2 jit_solution(2741359842075765459)
XLA Ops:
  1.3 19.1 %shard_map.85 = (f32[4,8,8,128]{3,2,1,0:T(8,128)S(1)}, f32[3,8,256]{2,1,0:T(8,128)S(1)}, f32[8,128]{1,0:T(8,128)S(1)}) custom-call(bf16[8,256,128]{2,1,0:T(8,128)(2,1)} %w_hbm.1, f32[8,256]{1,0:T(8,128)} %src_hbm.1, f32[8,256]{1,0:T(8,128)} %conf_hbm.1, s32[1,8]{1,0:T(1,128)} %bitcast.1, s32[3,8]{1,0:T(4,128)} %off_hbm.1, s32[1]{0:T(128)S(6)} %copy.9.count_hbm), custom_call_target="tpu_custom_call" | custom-call | tf_op jit(solution)/shard_map/pallas_call | solution.py:501
  20.4 0.8 %shard_map.86 = (f32[8,8,128]{2,1,0:T(8,128)}, f32[8,8,128]{2,1,0:T(8,128)}, f32[8,256]{1,0:T(8,128)}) custom-call(f32[4,8,8,128]{3,2,1,0:T(8,128)S(1)} %get-tuple-element.6.basis_ref, f32[3,8,256]{2,1,0:T(8,128)S(1)} %get-tuple-element.7.values_at, f32[8,128]{1,0:T(8,128)S(1)} %get-tuple-element.8.sums_ref), custom_call_target="tpu_custom_call" | custom-call | tf_op jit(solution)/shard_map/pallas_call | solution.py:546

commit v5 on v4

--- a/solution.py
+++ b/solution.py
@@ -96,7 +96,7 @@
            basis_ref, values_at, sums_ref,
            send, recv, zhot, xlow, xhigh, ylow, yhigh, zpack, halo_in,
            part, parts, colpart, colparts, back, returned, pay,
-           w_ref, src_ref, conf_ref, dest_ref, off_ref, in_s, one_s, one_r):
+           w_ref, src_ref, conf_ref, dest_ref, off_ref, one_s, one_r):
     nx, ny, nz, slots, cap = sizes
     group = ny * nz
     gx, gy, gz = lax.axis_index("gx"), lax.axis_index("gy"), lax.axis_index("gz")
@@ -138,7 +138,7 @@
         return ok
 
     loads = [
-        pltpu.make_async_copy(a, b, in_s.at[i])
+        pltpu.make_async_copy(a, b, one_s.at[i])
         for i, (a, b) in enumerate(
             (
                 (dest_hbm, dest_ref), (off_hbm, off_ref),
@@ -147,7 +147,7 @@
         )
     ]
     barrier = pltpu.get_barrier_semaphore()
-    for _, where in reversed(in_group):
+    for _, where in beyond + nearby:
         pl.semaphore_signal(barrier, inc=1, device_id=where, device_id_type=MESH)
     for c in loads:
         c.start()
@@ -204,7 +204,7 @@
 
     pl.semaphore_wait(barrier, len(in_group) + len(in_column))
     spread(0, nearby, lambda other: send.at[other], recv, me)
-    spread(5, beyond, lambda other: send.at[other], recv, me)
+    spread(3, beyond, lambda other: send.at[other], recv, me)
 
     cell = iota((BX * BY, 128), 1)
     place_xy = (iota((BX * BY, 128), 0) - (lax.shift_right_logical(cell, 5) * BY + (lax.shift_right_logical(cell, 3) & 3))).astype(F32)
@@ -247,7 +247,7 @@
     acc = jnp.zeros((4 * BX * BY, BZ), F32)
     if group <= 8:
         back_y, back_z = ([lax.rem(g + n - d, n) for d in range(n)] for g, n in ((gy, ny), (gz, nz)))
-        for first, kind, peers_of in ((0, 0, nearby), (1, 5, beyond)):
+        for first, kind, peers_of in ((0, 0, nearby), (1, 3, beyond)):
             if peers_of:
                 whole(kind, peers_of, recv).wait_recv()
             for y in range(ny):
@@ -255,7 +255,7 @@
                     acc = scatter(back_y[y] * nz + back_z[z], acc)
     else:
         whole(0, nearby, recv).wait_recv()
-        whole(5, beyond, recv).wait_recv()
+        whole(3, beyond, recv).wait_recv()
         acc = repeat(group, scatter, acc)
     both = acc[: 2 * BX * BY] + acc[2 * BX * BY :]
     rhs = both[: BX * BY].reshape(BX, BY, BZ)
@@ -323,7 +323,7 @@
     basis_ref[0] = rhs
     gather_of((rhs,), 0)
     whole(0, nearby, recv).wait_send()
-    whole(5, beyond, recv).wait_send()
+    whole(3, beyond, recv).wait_send()
     near = [jnp.minimum(g, 1) + jnp.minimum(n - 1 - g, 1) for g, n in ((gx, nx), (gy, ny), (gz, nz))]
     usual = [(0,) if n == 1 else (1,) if n == 2 else (1, 2) for n in (nx, ny, nz)]
 
@@ -450,14 +450,14 @@
     if not direct:
         colpart[...] = total
         colparts[gx] = total
-        spread(3, in_column, lambda other: colpart, colparts, gx)
-        whole(3, in_column, colparts).wait_recv()
+        spread(5, in_column, lambda other: colpart, colparts, gx)
+        whole(5, in_column, colparts).wait_recv()
         total = jnp.sum(colparts[...], axis=0)
     sums_ref[...] = jnp.where(own, jnp.broadcast_to(total, (8, 128)), 0.0)
     whole(1, peers, parts).wait_send()
     whole(2, in_group, returned).wait_send()
     if not direct:
-        whole(3, in_column, colparts).wait_send()
+        whole(5, in_column, colparts).wait_send()
 
 
 def finish(basis_ref, values_at, sums_ref, field_hbm, resid_hbm, point_hbm, field_ref, resid_ref, point_ref, out_s):
@@ -529,7 +529,7 @@
             pltpu.VMEM(confidence.shape, F32),
             pltpu.VMEM((1, slots), jnp.int32),
             pltpu.VMEM(offsets.shape, jnp.int32),
-            dma((6,)), dma((6,)), dma((6,)),
+            dma((5 if nx * group <= 64 else 6,)), dma((5 if nx * group <= 64 else 6,)),
         ],
         compiler_params=pltpu.CompilerParams(
             collective_id=0, has_side_effects=True, vmem_limit_bytes=40 * 1024 * 1024

time: 21.3 us -> 21.2 us (level)
  no operation moved by 1% of the time
where the time goes in v5:
time: 21.2 us; the launch traced here: 21 us
  Pallas kernels  19.7 us (93%)
  between operations  1.29 us (6%)
    pallas_call x1, Pallas kernels, shards(): pl.pallas_call(functools.partial(kernel, (nx, ny, nz, slots, cap)), out_s...  18.9 us
    pallas_call x1, Pallas kernels, shards(): pl.pallas_call(finish, out_shape=(brick, brick, jax.ShapeDtypeStruct((slo...  0.82 us

profile of v5, /device:TPU:0, one launch (start us, length us, event | category | flops | bytes accessed | tf_op | source)
XLA Modules:
  0.0 21.0 jit_solution(4530617024423800995)
XLA Ops:
  1.3 18.9 %shard_map.85 = (f32[4,8,8,128]{3,2,1,0:T(8,128)S(1)}, f32[3,8,256]{2,1,0:T(8,128)S(1)}, f32[8,128]{1,0:T(8,128)S(1)}) custom-call(bf16[8,256,128]{2,1,0:T(8,128)(2,1)} %w_hbm.1, f32[8,256]{1,0:T(8,128)} %src_hbm.1, f32[8,256]{1,0:T(8,128)} %conf_hbm.1, s32[1,8]{1,0:T(1,128)} %bitcast.1, s32[3,8]{1,0:T(4,128)} %off_hbm.1, s32[1]{0:T(128)S(6)} %copy.9.count_hbm), custom_call_target="tpu_custom_call" | custom-call | tf_op jit(solution)/shard_map/pallas_call | solution.py:501
  20.2 0.8 %shard_map.86 = (f32[8,8,128]{2,1,0:T(8,128)}, f32[8,8,128]{2,1,0:T(8,128)}, f32[8,256]{1,0:T(8,128)}) custom-call(f32[4,8,8,128]{3,2,1,0:T(8,128)S(1)} %get-tuple-element.6.basis_ref, f32[3,8,256]{2,1,0:T(8,128)S(1)} %get-tuple-element.7.values_at, f32[8,128]{1,0:T(8,128)S(1)} %get-tuple-element.8.sums_ref), custom_call_target="tpu_custom_call" | custom-call | tf_op jit(solution)/shard_map/pallas_call | solution.py:546

commit v6 on v5

--- a/solution.py
+++ b/solution.py
@@ -445,6 +445,8 @@
             at = v * slots + n
             values_at[v, n : n + 1, :] = out[at : at + 1] + out[ITERS * slots + at : ITERS * slots + at + 1]
 
+    whole(1, peers, parts).wait_send()
+    whole(2, in_group, returned).wait_send()
     whole(1, peers, parts).wait_recv()
     total = jnp.sum(parts[pl.ds(0, len(peers) + 1)], axis=0)
     if not direct:
@@ -454,8 +456,6 @@
         whole(5, in_column, colparts).wait_recv()
         total = jnp.sum(colparts[...], axis=0)
     sums_ref[...] = jnp.where(own, jnp.broadcast_to(total, (8, 128)), 0.0)
-    whole(1, peers, parts).wait_send()
-    whole(2, in_group, returned).wait_send()
     if not direct:
         whole(5, in_column, colparts).wait_send()
 
@@ -476,15 +476,14 @@
         return out
 
     field_ref[...] = combine(field_c)
-    copies[0].start()
     point = None
     for v, c in enumerate(field_c):
         term = jnp.concatenate([c] * (values_at.shape[2] // 128), 1) * values_at[v]
         point = term if point is None else point + term
     point_ref[...] = point
-    copies[1].start()
     resid_ref[...] = combine(resid_c)
-    copies[2].start()
+    for c in copies:
+        c.start()
     for c in copies:
         c.wait()
 

time: 21.2 us -> 21.2 us (level)
  no operation moved by 1% of the time
where the time goes in v6:
time: 21.2 us; the launch traced here: 21 us
  Pallas kernels  19.7 us (93%)
  between operations  1.29 us (6%)
    pallas_call x1, Pallas kernels, shards(): pl.pallas_call(functools.partial(kernel, (nx, ny, nz, slots, cap)), out_s...  18.9 us
    pallas_call x1, Pallas kernels, shards(): pl.pallas_call(finish, out_shape=(brick, brick, jax.ShapeDtypeStruct((slo...  0.82 us

profile of v6, /device:TPU:0, one launch (start us, length us, event | category | flops | bytes accessed | tf_op | source)
XLA Modules:
  0.0 21.0 jit_solution(10719641463800142285)
XLA Ops:
  1.3 18.9 %shard_map.85 = (f32[4,8,8,128]{3,2,1,0:T(8,128)S(1)}, f32[3,8,256]{2,1,0:T(8,128)S(1)}, f32[8,128]{1,0:T(8,128)S(1)}) custom-call(bf16[8,256,128]{2,1,0:T(8,128)(2,1)} %w_hbm.1, f32[8,256]{1,0:T(8,128)} %src_hbm.1, f32[8,256]{1,0:T(8,128)} %conf_hbm.1, s32[1,8]{1,0:T(1,128)} %bitcast.1, s32[3,8]{1,0:T(4,128)} %off_hbm.1, s32[1]{0:T(128)S(6)} %copy.9.count_hbm), custom_call_target="tpu_custom_call" | custom-call | tf_op jit(solution)/shard_map/pallas_call | solution.py:500
  20.2 0.8 %shard_map.86 = (f32[8,8,128]{2,1,0:T(8,128)}, f32[8,8,128]{2,1,0:T(8,128)}, f32[8,256]{1,0:T(8,128)}) custom-call(f32[4,8,8,128]{3,2,1,0:T(8,128)S(1)} %get-tuple-element.6.basis_ref, f32[3,8,256]{2,1,0:T(8,128)S(1)} %get-tuple-element.7.values_at, f32[8,128]{1,0:T(8,128)S(1)} %get-tuple-element.8.sums_ref), custom_call_target="tpu_custom_call" | custom-call | tf_op jit(solution)/shard_map/pallas_call | solution.py:545
